TPU v7x, 32 devices: a whole 2x2x4 slice. The times are simulated.
32 devices in a mesh: row: 4 (over y, core), col: 8 (over z, x).
Axes of the slice: x: 2, y: 2, z: 4, core: 2. Of those that a mesh axis runs over, the one named last changes fastest.
Arguments:
- positions: float32 [32, 3, 1024], P(None, None, ('row', 'col')), may hold values from -1 to 25, as said below
- charges: float32 [1024], P(('row', 'col')), may hold values from -3 to 3
- atom_types: int32 [1024], P(('row', 'col')), may hold values from 0 to 31
- exclusions: int32 [1024], P('row'), may hold values from 0 to 1073741823, as said below
- type_radius: float32 [32], replicated, may hold values from 1.1 to 2
- type_volume: float32 [32], replicated, may hold values from 0.03 to 0.3
Outputs:
- forces: float32 [32, 3, 1024], P(None, None, ('row', 'col'))
- born_radii: float32 [32, 1024], P(None, ('row', 'col'))
Inputs may be any that keep to these rules, and one draw needn't show every extreme that they name: `positions`: within one conformation no two atoms are closer than 0.8. Bit k (k < 15) of exclusions[a] marks the pair a, a + k + 1 and bit 15 + k marks the pair a, a - k - 1; the two marks of one pair agree, and no bit names an atom outside 0 to 1023.
All inputs are finite; a program needn't handle non-finite values.
Results may differ from a plain program's by a relative error of at most 0.0003.
Values sent between devices are 32-bit elements; how exact they have to be, the bound alone decides.
No kernel may reach another device: no remote copies, remote signals or barrier semaphores. Data moves between devices by JAX's collectives and lax.ppermute only.
A program may use at most 64 MiB of HBM per device.

v0:
```python
from functools import partial
import math

import jax
import jax.numpy as jnp
from jax import lax
from jax.sharding import PartitionSpec as P

SOLVENT_FACTOR = 1.0 - 1.0 / 78.5


def geometry(rowrep, colrep):
    displace = rowrep[0:3, :, :, None] - colrep[0:3, :, None, :]
    distsq = jnp.sum(displace * displace, axis=0)
    return (displace, distsq)


def pair_masks(row_ids, col_ids, masks):
    shift_gap = col_ids[None, :] - row_ids[:, None]
    holder = masks[:, None]
    paired = shift_gap != 0
    nearby = paired & (jnp.abs(shift_gap) <= 15)
    bitpos = jnp.where(shift_gap > 0, shift_gap - 1, 14 - shift_gap)
    bitpos = jnp.where(nearby, bitpos, 0)
    bitflag = jnp.bitwise_and(jnp.right_shift(holder, bitpos), 1)
    excluded = nearby & (bitflag == 1)
    weight = jnp.where(paired & jnp.logical_not(excluded), 1.0, 0.0).astype(jnp.float32)
    return (weight, paired)


def coulomb_grad(displace, distsq, rowatom, colatom, weight, paired):
    guarded = jnp.where(paired[None], distsq, 1.0)
    inverse = lax.rsqrt(guarded)
    factor = (
        -(weight * rowatom[0][:, None] * colatom[0][None, :])[None] * inverse * inverse * inverse
    )
    return jnp.sum(factor[None] * displace, axis=3)


def descreen_kernel(rowrep, colrep, rowatom, colatom, row_ids, col_ids, masks, on_rows, coul_first):
    displace, distsq = geometry(rowrep, colrep)
    weight, paired = pair_masks(row_ids, col_ids, masks)
    denom = distsq + (colatom[2] * colatom[2])[None, None, :]
    inverse = 1.0 / denom
    descreen = jnp.where(paired[None], colatom[1][None, None, :] * inverse * inverse, 0.0)
    pieces = jnp.sum(descreen, axis=2)[None]
    return pieces


def born_kernel(rowrep, colrep, rowatom, colatom, row_ids, col_ids, masks, on_rows, coul_last):
    displace, distsq = geometry(rowrep, colrep)
    radius_row = rowrep[3][:, :, None]
    radius_col = colrep[3][:, None, :]
    product = radius_row * radius_col
    damping = jnp.exp(-distsq / (4.0 * product))
    effective = distsq + product * damping
    reciprocal = lax.rsqrt(effective)
    cubed = reciprocal * reciprocal * reciprocal
    charge_pair = SOLVENT_FACTOR * (rowatom[0][:, None] * colatom[0][None, :])[None]
    direct = jnp.sum((charge_pair * cubed * (1.0 - 0.25 * damping))[None] * displace, axis=3)
    radial = jnp.sum(
        0.5 * charge_pair * cubed * damping * (1.0 + distsq / (4.0 * product)) * radius_col, axis=2
    )
    pieces = [radial[None], direct]
    weight, paired = pair_masks(row_ids, col_ids, masks)
    pieces.append(coulomb_grad(displace, distsq, rowatom, colatom, weight, paired))
    return jnp.concatenate(pieces, axis=0)


def chain_kernel(rowrep, colrep, rowatom, colatom, row_ids, col_ids, masks, on_rows):
    displace, distsq = geometry(rowrep, colrep)
    weight, paired = pair_masks(row_ids, col_ids, masks)
    inv_row = 1.0 / (distsq + (rowatom[2] * rowatom[2])[None, :, None])
    inv_col = 1.0 / (distsq + (colatom[2] * colatom[2])[None, None, :])
    factor = rowrep[3][:, :, None] * colatom[1][None, None, :] * inv_col * inv_col * inv_col
    factor = (
        factor + colrep[3][:, None, :] * rowatom[1][None, :, None] * inv_row * inv_row * inv_row
    )
    factor = jnp.where(paired[None], -4.0 * factor, 0.0)
    return jnp.sum(factor[None] * displace, axis=3)


def radii(radius, integral):
    saturation = jnp.tanh(radius * integral)
    born = 1.0 / (1.0 / radius - saturation / (radius + 0.09))
    slope = born * born * (1.0 - saturation * saturation) * radius / (radius + 0.09)
    return (born, slope)


def run_pass(kernel, rowrep, colrep, rowatom, colatom, row_ids, col_ids, masks, fields):
    planes, replicas, row_len = rowrep.shape
    col_len = colrep.shape[2]
    group = math.gcd(replicas, 8)
    groups = replicas // group
    tile_len = 128
    tiles = col_len // tile_len
    row_groups = rowrep.reshape(planes, groups, group, row_len).transpose(1, 0, 2, 3)
    col_groups = colrep.reshape(planes, groups, group, tiles, tile_len).transpose(1, 3, 0, 2, 4)
    col_atoms = colatom.reshape(colatom.shape[0], tiles, tile_len).transpose(1, 0, 2)
    col_tiles = col_ids.reshape(tiles, tile_len)

    def one_group(inputs):
        row_block, col_block = inputs

        def advance(running, pieces):
            col_tile, atom_tile, id_tile = pieces
            return (
                running
                + kernel(row_block, col_tile, rowatom, atom_tile, row_ids, id_tile, masks, True),
                None,
            )

        scanned = (col_block, col_atoms, col_tiles)
        start = jnp.zeros((fields, group, row_len), jnp.float32)
        running, _ = lax.scan(advance, start, scanned)
        return running

    result = lax.map(one_group, (row_groups, col_groups))
    return result.transpose(1, 0, 2, 3).reshape(fields, replicas, row_len)


def along_rows(packed):
    return lax.all_gather(packed, "col", axis=1, tiled=True)


def along_cols(packed):
    return lax.all_gather(packed, "row", axis=1, tiled=True)


def fold_own(terms):
    return lax.psum_scatter(terms, "col", scatter_dimension=2, tiled=True)


def on_device(positions, charges, atom_types, exclusions, type_radius, type_volume):
    replicas = positions.shape[0]
    owned = positions.shape[2]
    row_count = lax.axis_size("row")
    col_count = lax.axis_size("col")
    row_index = lax.axis_index("row")
    col_index = lax.axis_index("col")
    row_len = owned * col_count
    col_len = owned * row_count
    type_ids = jnp.arange(type_radius.shape[0], dtype=jnp.int32)
    onehot = (atom_types[:, None] == type_ids[None, :]).astype(jnp.float32)
    radius = jnp.sum(onehot * type_radius[None, :], axis=1)
    volume = jnp.sum(onehot * type_volume[None, :], axis=1)
    owned_pack = jnp.concatenate(
        [
            positions.transpose(1, 0, 2).reshape(3 * replicas, owned),
            charges[None],
            volume[None],
            radius[None],
        ],
        axis=0,
    )
    row_pack = along_rows(owned_pack)
    col_pack = along_cols(owned_pack)
    row_pos = row_pack[: 3 * replicas].reshape(3, replicas, row_len)
    row_atom = row_pack[3 * replicas :]
    col_pos = col_pack[: 3 * replicas].reshape(3, replicas, col_len)
    col_atom = col_pack[3 * replicas :]
    row_ids = row_index * row_len + jnp.arange(row_len, dtype=jnp.int32)
    col_ids = (
        (jnp.arange(row_count, dtype=jnp.int32)[:, None] * col_count + col_index) * owned
        + jnp.arange(owned, dtype=jnp.int32)[None, :]
    ).reshape(col_len)

    def pair_pass(kernel, fields, row_rep, col_rep):
        return run_pass(
            kernel, row_rep, col_rep, row_atom, col_atom, row_ids, col_ids, exclusions, fields
        )

    first_fields = 1
    first = pair_pass(partial(descreen_kernel, coul_first=False), first_fields, row_pos, col_pos)
    first_own = fold_own(first)
    born, slope = radii(radius[None, :], first_own[0])
    born_rows = along_rows(born)
    born_cols = along_cols(born)
    second_fields = 7
    row_born = jnp.concatenate([row_pos, born_rows[None]], axis=0)
    col_born = jnp.concatenate([col_pos, born_cols[None]], axis=0)
    second = pair_pass(partial(born_kernel, coul_last=True), second_fields, row_born, col_born)
    second_own = fold_own(second)
    chained = second_own[0] * slope
    chain_rows = along_rows(chained)
    chain_cols = along_cols(chained)
    row_chain = jnp.concatenate([row_pos, chain_rows[None]], axis=0)
    col_chain = jnp.concatenate([col_pos, chain_cols[None]], axis=0)
    third = pair_pass(chain_kernel, 3, row_chain, col_chain)
    third_own = fold_own(third)
    coulomb_own = second_own[4:7]
    gradient = second_own[1:4] + coulomb_own + third_own
    forces = (-gradient).transpose(1, 0, 2)
    return (forces, born)


def solution(mesh):
    return jax.shard_map(
        on_device,
        mesh=mesh,
        in_specs=(
            P(None, None, ("row", "col")),
            P(("row", "col")),
            P(("row", "col")),
            P("row"),
            P(),
            P(),
        ),
        out_specs=(P(None, None, ("row", "col")), P(None, ("row", "col"))),
        check_vma=False,
    )
```

profile of v0, /device:TPU:0, one launch (start us, length us, event | category | flops | bytes accessed | tf_op | source)
XLA Modules:
  0.0 363.6 jit_solution(15120952996015415024)
XLA Ops:
  7.2 0.9 select_reduce_fusion.1
  8.3 0.9 copy.115
  9.1 0.8 copy.79
  10.0 6.2 %all_gather.19 = f32[99,128]{0,1:T(8,128)S(1)} all-gather(f32[99,32]{0,1:T(8,128)S(1)} %pad_maximum_fusion.4), channel_id=1, replica_groups=mesh['row'=4,'col'=8] {'row'}, dimensions={1}, use_global_device_ids=true | all-gather | bytes 63360 | tf_op jit(solution)/shard_map/all_gather | solution.py:127
  16.3 0.1 slice_multiply_fusion.1
  16.4 31.4 %all_gather.18 = f32[99,256]{0,1:T(8,128)S(1)} all-gather(f32[99,32]{0,1:T(8,128)S(1)} %pad_maximum_fusion.4), channel_id=1, replica_groups=mesh['row'=4,'col'=8] {'col'}, dimensions={1}, use_global_device_ids=true | all-gather | bytes 114048 | tf_op jit(solution)/shard_map/all_gather | solution.py:123
  47.9 0.1 copy.122
  48.0 7.0 %while.49 = (s32[]{:T(128)}, f32[4,1,8,256]{3,2,1,0:T(8,128)S(1)}, f32[1,3,128]{2,1,0:T(4,128)S(1)}, f32[4,3,8,256]{3,2,0,1:T(8,128)S(1)}, f32[4,1,3,8,128]{4,3,...) while((s32[]{:T(128)}, f32[4,1,8,256]{3,2,1,0:T(8,128)S(1)}, ...), condition=%wide.region_5.6_spmd.clone, body=%wide.region_2.5_spmd.clone.sunk | while | flops 3733890 | bytes 2304133 | solution.py:118
  48.4 1.0 multiply_reduce_fusion.2
  49.4 0.4 fusion.59
  50.1 1.0 multiply_reduce_fusion.2
  51.2 0.4 fusion.59
  51.7 0.1 subtract_compare_fusion.7
  51.8 1.0 multiply_reduce_fusion.2
  52.9 0.4 fusion.59
  53.6 1.0 multiply_reduce_fusion.2
  54.6 0.4 fusion.59
  55.0 0.7 copy.109
  56.1 62.1 %reduce-scatter.10.cloned.1.call-done = f32[32,32]{1,0:T(8,128)} async-done(((f32[256,32]{1,0:T(8,128)}), f32[32,32]{1,0:T(8,128)}) %reduce-scatter.10.cloned.1.call-update) | async-done | bytes 4112
  118.1 0.8 copy.110
  119.0 5.2 %all_gather.21 = f32[32,128]{0,1:T(8,128)S(1)} all-gather(f32[32,32]{0,1:T(8,128)S(1)} %copy.88), channel_id=1, replica_groups=mesh['row'=4,'col'=8] {'row'}, dimensions={1}, use_global_device_ids=true | all-gather | bytes 20480 | tf_op jit(solution)/shard_map/all_gather | solution.py:127
  124.3 30.5 %all_gather.20 = f32[32,256]{0,1:T(8,128)S(1)} all-gather(f32[32,32]{0,1:T(8,128)S(1)} %copy.88), channel_id=1, replica_groups=mesh['row'=4,'col'=8] {'col'}, dimensions={1}, use_global_device_ids=true | all-gather | bytes 36864 | tf_op jit(solution)/shard_map/all_gather | solution.py:123
  155.0 23.8 %while.50 = (s32[]{:T(128)}, f32[4,7,8,256]{3,2,1,0:T(8,128)S(1)}, f32[3,256]{1,0:T(4,128)S(1)}, f32[1,3,128]{2,1,0:T(4,128)S(1)}, f32[4,4,8,256]{3,2,0,1:T(8,12...) while((s32[]{:T(128)}, f32[4,7,8,256]{3,2,1,0:T(8,128)S(1)}, ...), condition=%wide.region_12.13_spmd.clone, body=%wide.region_7.12_spmd.clone.sunk | while | flops 12892546 | bytes 7609485 | solution.py:118
  155.3 0.2 multiply_multiply_fusion.10
  155.6 1.0 fusion.60
  156.6 1.5 fusion.61
  158.1 2.8 fusion.62
  161.3 0.2 multiply_multiply_fusion.10
  161.5 1.0 fusion.60
  162.6 1.5 fusion.61
  164.1 2.8 fusion.62
  167.2 0.2 multiply_multiply_fusion.10
  167.5 1.0 fusion.60
  168.5 1.5 fusion.61
  170.0 2.8 fusion.62
  173.2 0.2 multiply_multiply_fusion.10
  173.4 1.0 fusion.60
  174.5 1.5 fusion.61
  176.0 2.8 fusion.62
  178.8 0.4 copy.111
  179.2 1.0 reshape.443
  180.3 0.2 fusion.44
  180.5 60.6 %reduce-scatter.12.cloned.1.call-done = f32[32,224]{1,0:T(8,128)} async-done(((f32[256,224]{1,0:T(8,128)}), f32[32,224]{1,0:T(8,128)}) %reduce-scatter.12.cloned.1.call-update) | async-done | bytes 28688
  241.1 0.8 reshape.444
  242.1 5.2 %all_gather.23 = f32[32,128]{0,1:T(8,128)S(1)} all-gather(f32[32,32]{0,1:T(8,128)S(1)} %copy.98), channel_id=1, replica_groups=mesh['row'=4,'col'=8] {'row'}, dimensions={1}, use_global_device_ids=true | all-gather | bytes 20480 | tf_op jit(solution)/shard_map/all_gather | solution.py:127
  247.4 30.5 %all_gather.22 = f32[32,256]{0,1:T(8,128)S(1)} all-gather(f32[32,32]{0,1:T(8,128)S(1)} %copy.98), channel_id=1, replica_groups=mesh['row'=4,'col'=8] {'col'}, dimensions={1}, use_global_device_ids=true | all-gather | bytes 36864 | tf_op jit(solution)/shard_map/all_gather | solution.py:123
  278.0 15.8 %while.51 = (s32[]{:T(128)}, f32[4,3,8,256]{3,2,1,0:T(8,128)S(1)}, f32[4,4,8,256]{3,2,0,1:T(8,128)S(1)}, f32[1,3,128]{2,1,0:T(4,128)S(1)}, f32[4,1,4,8,128]{4,3,...) while((s32[]{:T(128)}, f32[4,3,8,256]{3,2,1,0:T(8,128)S(1)}, ...), condition=%wide.region_17.18_spmd.clone, body=%wide.region_14.17_spmd.clone.sunk | while | flops 8448386 | bytes 4626581 | solution.py:118
  278.4 1.0 fusion.64
  279.5 0.6 fusion.65
  280.1 1.9 fusion.66
  282.4 1.0 fusion.64
  283.4 0.6 fusion.65
  284.0 1.9 fusion.66
  286.3 1.0 fusion.64
  287.4 0.6 fusion.65
  288.0 1.9 fusion.66
  290.3 1.0 fusion.64
  291.3 0.6 fusion.65
  291.9 1.9 fusion.66
  293.9 0.2 copy.113
  294.1 0.9 reshape.445
  295.2 60.3 %reduce-scatter.14.cloned.1.call-done = f32[32,96]{1,0:T(8,128)} async-done(((f32[256,96]{1,0:T(8,128)}), f32[32,96]{1,0:T(8,128)}) %reduce-scatter.14.cloned.1.call-update) | async-done | bytes 12304
  355.5 0.8 reshape.446
  356.4 0.6 negate_bitcast_fusion
  (179 shorter events, 5.3 us)
Async XLA Ops:
  7.2 111.0 %reduce-scatter.10.cloned.1.call-start = ((), (), s32[]{:S(2)}) async-start(), calls=%async_computation.3 | async-start | bytes 147456
  55.0 99.9 %copy-start.1 = (s32[256]{0:T(256)S(1)}, s32[256]{0:T(256)}, u32[]{:S(2)}) copy-start(s32[256]{0:T(256)} %param.15) | copy-start | bytes 3076
  55.8 185.3 %reduce-scatter.12.cloned.1.call-start = ((), (), s32[]{:S(2)}) async-start(), calls=%async_computation.4 | async-start | bytes 294912
  119.0 36.0 %copy-start = (f32[32,32]{1,0:T(8,128)}, f32[32,32]{1,0:T(8,128)S(1)}, u32[]{:S(2)}) copy-start(f32[32,32]{1,0:T(8,128)S(1)} %subtract_divide_fusion) | copy-start | bytes 12292
  180.2 175.3 %reduce-scatter.14.cloned.1.call-start = ((), (), s32[]{:S(2)}) async-start(), calls=%async_computation.5 | async-start | bytes 147456
Sparse Core Ops, SparseCore 0:
  55.9 62.1 reduce-scatter.9
  180.4 60.6 reduce-scatter.11
  295.1 60.3 reduce-scatter.13
where the time goes:
time: 364 us
  waiting for transfers between devices  183 us (50%)
  blocking collectives  109 us (30%)
  other arithmetic  46.1 us (13%)
  between operations  14 us (4%)
  local copies, waits for them, and re-layouts  10.2 us (3%)
    unnamed x6, waiting for transfers between devices  183 us
    all_gather x3, blocking collectives, along_rows(): return lax.all_gather(packed, 'col', axis=1, tiled=True)  92.4 us
    all_gather x3, blocking collectives, along_cols(): return lax.all_gather(packed, 'row', axis=1, tiled=True)  16.7 us
    reduce_sum x12, other arithmetic, geometry(): distsq = jnp.sum(displace * displace, axis=0)  12.6 us
    reduce_sum x4, other arithmetic, born_kernel(): jnp.sum((charge_pair * cubed * (1.0 - 0.25 * damping))[None] * displace,...  11.2 us
    reduce_sum x4, other arithmetic, chain_kernel(): return jnp.sum(factor[None] * displace, axis=3)  7.64 us
  transfers between devices with their start and end apart: 3, of which 3 were waited for; matrix products, arithmetic and copies ran while one was open for 0% of the time, Pallas kernels for 0%

commit v1 on v0

v1 whole, which is shorter than its diff:
```python
from functools import partial
import math

import jax
import jax.numpy as jnp
from jax import lax
from jax.experimental import pallas as pl
from jax.experimental.pallas import tpu as pltpu
from jax.sharding import PartitionSpec as P

SOLVENT_FACTOR = 1.0 - 1.0 / 78.5
LANES = 128
SUBLANES = 8
BAND = 15


TURNS = 64
TOGETHER = 21
X, Y, Z, Q, RHO2, VOL, BORN, DECAY, QBORN, CHAIN = range(10)


def pack_kernel(positions_any, charges_any, types_any, marks_any, radius_any, volume_any, out_ref,
                positions, charges, types, marks, radius, volume, arrived):
    moves = []
    for n, (source, target) in enumerate(
        (
            (positions_any, positions),
            (charges_any, charges),
            (types_any, types),
            (marks_any, marks),
            (radius_any, radius),
            (volume_any, volume),
        )
    ):
        moves.append(pltpu.make_async_copy(source, target, arrived.at[n]))
        moves[-1].start()
    for move in moves:
        move.wait()
    replicas, owned = positions.shape[1:]

    def widened(line):
        line = jnp.concatenate([line, jnp.zeros((1, LANES - line.shape[1]), line.dtype)], axis=1)
        return jnp.broadcast_to(line, (SUBLANES, LANES))

    kinds = widened(types[...])

    def look_up(table):
        return jnp.take_along_axis(widened(table[...]), kinds, axis=1, mode="promise_in_bounds")[0:1, :owned]

    per = LANES // owned
    column = lax.axis_index("col")
    forward = jnp.bitwise_and(marks[...], (1 << BAND) - 1).astype(jnp.float32)
    line = lax.broadcasted_iota(jnp.int32, forward.shape, 0)
    picked = jnp.sum(jnp.where(line == lax.div(column, per), forward, 0.0), axis=0, keepdims=True)
    shift = lax.rem(LANES - lax.rem(column, per) * owned, LANES)
    picked = pltpu.roll(jnp.broadcast_to(picked, (SUBLANES, LANES)), shift, 1)[0:1, :owned]

    def everywhere(row):
        return jnp.broadcast_to(row, (replicas, owned))

    first = [positions[0], positions[1], positions[2], everywhere(charges[...])]
    second = [everywhere(look_up(radius)), everywhere(look_up(volume)), everywhere(picked), jnp.zeros((replicas, owned), jnp.float32)]
    out_ref[pl.ds(0, replicas, stride=2), :] = jnp.concatenate(first, axis=1)
    out_ref[pl.ds(1, replicas, stride=2), :] = jnp.concatenate(second, axis=1)


def pack(positions, charges, atom_types, exclusions, type_radius, type_volume):
    replicas, _, owned = positions.shape
    lines = exclusions.shape[0] // LANES
    anywhere = pl.BlockSpec(memory_space=pl.ANY)
    return pl.pallas_call(
        pack_kernel,
        out_shape=jax.ShapeDtypeStruct((replicas * 2, LANES), jnp.float32),
        in_specs=[anywhere] * 6,
        out_specs=pl.BlockSpec(memory_space=pltpu.VMEM),
        scratch_shapes=[
            pltpu.VMEM((3, replicas, owned), jnp.float32),
            pltpu.VMEM((1, owned), jnp.float32),
            pltpu.VMEM((1, owned), jnp.int32),
            pltpu.VMEM((lines, LANES), jnp.int32),
            pltpu.VMEM((1,) + type_radius.shape, jnp.float32),
            pltpu.VMEM((1,) + type_volume.shape, jnp.float32),
            pltpu.SemaphoreType.DMA((6,)),
        ],
        compiler_params=pltpu.CompilerParams(vmem_limit_bytes=60 * 1024 * 1024),
    )(
        positions.transpose(1, 0, 2),
        charges[None],
        atom_types[None],
        exclusions.reshape(lines, LANES),
        type_radius[None],
        type_volume[None],
    )


def conformation_kernel(recv_ref, out_ref, turned, moved, shown, backs, pair_a, pair_b, pair_c, pair_d):
    owners = out_ref.shape[0]
    per = owners // SUBLANES
    owned = LANES // per
    shape = (SUBLANES, LANES)
    half = SUBLANES // 2

    def dense(k):
        part, first = k // per, k % per * owned
        rows = [recv_ref[pl.ds(2 * j + part, SUBLANES, stride=2 * per), :] for j in range(per)]
        return jnp.concatenate([row[:, first : first + owned] for row in rows], axis=1)

    def keep(k, value, move=None):
        for drop in range(SUBLANES):
            turned[k, drop] = pltpu.roll(value, drop, 0) if drop else value
        move = value if move is None else move
        for turn in range(TURNS + 1):
            moved[k, turn] = pltpu.roll(move, turn, 1) if turn else move

    x, y, z, q, rho, vol, marks = [dense(k) for k in range(7)]
    for k, value in ((X, x), (Y, y), (Z, z), (RHO2, rho * rho), (VOL, vol)):
        keep(k, value)
    zero = jnp.zeros(shape, jnp.float32)
    one = jnp.ones(shape, jnp.float32)

    def sweep(pair, names, fields):
        def block(first, turns, drops, stay, two_sided=range(SUBLANES)):
            stayer = {drop: {k: turned[k, drop] for k in names} for drop in drops}
            stay = [list(line) for line in stay]
            for t in range(turns):
                turn = first + t
                mover = {k: moved[k, turn] for k in names}
                back = None
                for n, drop in enumerate(drops):
                    to_mover, to_stayer = pair(mover, stayer[drop], turn, drop)
                    stay[n] = [a + b for a, b in zip(stay[n], to_stayer)]
                    if drop in two_sided:
                        back = to_mover if back is None else [a + b for a, b in zip(back, to_mover)]
                if back is not None:
                    for k in range(fields):
                        backs[k, drops[0] // half, turn] = back[k]
            return stay

        total = [[zero] * 4 for _ in range(fields)]
        for part in range(2):
            drops = list(range(part * half, (part + 1) * half))
            stay = [[zero] * fields for _ in drops]
            for turn in (0, TURNS):
                edge = drops if part == 0 else drops[:1]
                stay[: len(edge)] = block(turn, 1, edge, stay[: len(edge)], two_sided=range(1, half))

            def steps(i, state):
                return block(i * TOGETHER + 1, TOGETHER, drops, state)

            stay = lax.fori_loop(0, (TURNS - 1) // TOGETHER, steps, stay)
            for n, drop in enumerate(drops):
                for k in range(fields):
                    total[k][n] = total[k][n] + (pltpu.roll(stay[n][k], SUBLANES - drop, 0) if drop else stay[n][k])
        for k in range(fields):
            for turn in range(TURNS + 1):
                back = backs[k, 0, turn]
                if turn not in (0, TURNS):
                    back = back + backs[k, 1, turn]
                total[k][turn % 4] = total[k][turn % 4] + (pltpu.roll(back, LANES - turn, 1) if turn else back)
        return [(t[0] + t[1]) + (t[2] + t[3]) for t in total]

    def itself(turn, drop):
        return isinstance(turn, int) and turn == 0 and drop == 0

    def descreen(mover, stayer, turn, drop):
        dx, dy, dz = [mover[k] - stayer[k] for k in (X, Y, Z)]
        distsq = dx * dx + dy * dy + dz * dz
        inv_mover = pltpu.reciprocal(distsq + mover[RHO2], approx=True)
        inv_stayer = pltpu.reciprocal(distsq + stayer[RHO2], approx=True)
        from_mover = mover[VOL] * (inv_mover * inv_mover)
        from_stayer = stayer[VOL] * (inv_stayer * inv_stayer)
        pair_a[turn, drop] = distsq
        pair_b[turn, drop] = from_mover * inv_mover
        pair_c[turn, drop] = from_stayer * inv_stayer
        if itself(turn, drop):
            return [zero], [zero]
        return [from_stayer], [from_mover]

    (integral,) = sweep(descreen, (X, Y, Z, RHO2, VOL), 1)
    saturation = jnp.tanh(rho * integral)
    born = 1.0 / (1.0 / rho - saturation / (rho + 0.09))
    slope = born * born * (1.0 - saturation * saturation) * rho / (rho + 0.09)
    decay = (math.sqrt(math.log2(math.e)) / 2.0) / born
    keep(BORN, born)
    keep(DECAY, decay, -decay)
    keep(QBORN, q * born)

    def born_terms(mover, stayer, turn, drop):
        distsq = pair_a[turn, drop]
        power = distsq * (mover[DECAY] * stayer[DECAY])
        damping = jnp.exp2(power)
        effective = distsq + (mover[BORN] * stayer[BORN]) * damping
        cubed = lax.rsqrt(effective) * pltpu.reciprocal(effective, approx=True)
        pair_d[turn, drop] = cubed * (SOLVENT_FACTOR - (0.25 * SOLVENT_FACTOR) * damping)
        radial = cubed * (damping * (1.0 / math.log(2.0) - power))
        return [radial * stayer[QBORN]], [radial * mover[QBORN]]

    (radial,) = sweep(born_terms, (BORN, DECAY, QBORN), 1)
    chained = (0.5 * SOLVENT_FACTOR * math.log(2.0)) * q * radial * slope
    keep(CHAIN, 4.0 * chained)
    keep(Q, q)
    marks = marks.astype(jnp.int32)
    lane = lax.broadcasted_iota(jnp.int32, shape, 1)
    for turn in range(1, TURNS):
        if turn <= BAND:
            marked = jnp.bitwise_and(jnp.right_shift(pltpu.roll(marks, turn, 1), turn - 1), 1) == 1
            shown[turn, 0] = jnp.where(marked & (lane >= turn), 0.0, 1.0)
            shown[turn, 1] = jnp.where(marked & (lane < turn), 0.0, 1.0)
        else:
            shown[turn, 0] = one
            shown[turn, 1] = one

    def force_terms(mover, stayer, turn, drop):
        if itself(turn, drop):
            return [zero] * 3, [zero] * 3
        distsq = pair_a[turn, drop]
        bare = lax.rsqrt(distsq) * pltpu.reciprocal(distsq, approx=True)
        if drop in (0, SUBLANES - 1) and not isinstance(turn, int):
            bare = bare * shown[turn, min(drop, 1)]
        chain = stayer[CHAIN] * pair_b[turn, drop] + mover[CHAIN] * pair_c[turn, drop]
        factor = chain + (bare - pair_d[turn, drop]) * (mover[Q] * stayer[Q])
        push = [factor * (mover[k] - stayer[k]) for k in (X, Y, Z)]
        return push, [-p for p in push]

    results = sweep(force_terms, (X, Y, Z, Q, CHAIN), 3) + [born]
    for j in range(per):
        out_ref[pl.ds(j, SUBLANES, stride=per), :] = jnp.concatenate(
            [value[:, j * owned : (j + 1) * owned] for value in results], axis=1
        )


def whole_conformation(recv):
    vmem = pl.BlockSpec(memory_space=pltpu.VMEM)
    dense = (SUBLANES, LANES)
    kept = pltpu.VMEM((TURNS + 1, SUBLANES) + dense, jnp.float32)
    return pl.pallas_call(
        conformation_kernel,
        out_shape=jax.ShapeDtypeStruct((recv.shape[0] // 2, LANES), jnp.float32),
        in_specs=[vmem],
        out_specs=vmem,
        scratch_shapes=[
            pltpu.VMEM((10, SUBLANES) + dense, jnp.float32),
            pltpu.VMEM((10, TURNS + 1) + dense, jnp.float32),
            pltpu.VMEM((TURNS, 2) + dense, jnp.float32),
            pltpu.VMEM((3, 2, TURNS + 1) + dense, jnp.float32),
            kept,
            kept,
            kept,
            kept,
        ],
        compiler_params=pltpu.CompilerParams(vmem_limit_bytes=32 * 1024 * 1024),
    )(recv)


def unpack_kernel(back_ref, forces_any, born_any, forces, born, sent):
    owned = born.shape[1]
    born[...] = back_ref[:, 3 * owned : 4 * owned]
    moves = [pltpu.make_async_copy(born, born_any, sent.at[3])]
    moves[0].start()
    for axis in range(3):
        forces[axis] = back_ref[:, axis * owned : (axis + 1) * owned]
        moves.append(pltpu.make_async_copy(forces.at[axis], forces_any.at[axis], sent.at[axis]))
        moves[-1].start()
    for move in moves:
        move.wait()


def unpack(back):
    replicas, width = back.shape
    owned = width // 4
    forces = ((3, replicas, owned), jnp.float32)
    born = ((replicas, owned), jnp.float32)
    anywhere = pl.BlockSpec(memory_space=pl.ANY)
    forces, born = pl.pallas_call(
        unpack_kernel,
        out_shape=[jax.ShapeDtypeStruct(*forces), jax.ShapeDtypeStruct(*born)],
        in_specs=[pl.BlockSpec(memory_space=pltpu.VMEM)],
        out_specs=[anywhere, anywhere],
        scratch_shapes=[pltpu.VMEM(*forces), pltpu.VMEM(*born), pltpu.SemaphoreType.DMA((4,))],
    )(back)
    return (forces.transpose(1, 0, 2), born)


def shared_sum(kernel, own, everyone, fields):
    conformations, planes, count = everyone.shape
    tiles = count // LANES
    tiled = everyone.reshape(conformations, planes, tiles, LANES).transpose(2, 0, 1, 3)
    ids = jnp.arange(count, dtype=jnp.int32).reshape(tiles, LANES)

    def advance(running, piece):
        return (running + kernel(own, *piece), None)

    start = jnp.zeros((fields, conformations, own[0].shape[2]), jnp.float32)
    return lax.scan(advance, start, (tiled, ids))[0]


def split_pair(own, tile):
    atoms = [own[0][:, k, :, None] for k in range(own[0].shape[1])]
    others = [tile[:, k, None, :] for k in range(tile.shape[1])]
    displace = jnp.stack([atoms[k] - others[k] for k in range(3)])
    return (atoms, others, displace, jnp.sum(displace * displace, axis=0))


def shared_descreen(own, tile, ids):
    atoms, others, displace, distsq = split_pair(own, tile)
    inverse = 1.0 / (distsq + others[4] * others[4])
    terms = jnp.where(own[1][:, None] != ids[None, :], others[5] * inverse * inverse, 0.0)
    return jnp.sum(terms, axis=2)[None]


def shared_born(own, tile, ids):
    atoms, others, displace, distsq = split_pair(own, tile)
    gap = ids[None, :] - own[1][:, None]
    nearby = (gap != 0) & (jnp.abs(gap) <= BAND)
    position = jnp.where(nearby, jnp.where(gap > 0, gap - 1, BAND - 1 - gap), 0)
    marked = jnp.bitwise_and(jnp.right_shift(own[2][:, None], position), 1) == 1
    weight = jnp.where((gap == 0) | (nearby & marked), 0.0, 1.0)
    bare = lax.rsqrt(jnp.where(gap == 0, 1.0, distsq))
    product = atoms[6] * others[6]
    power = distsq / (4.0 * product)
    damping = jnp.exp(-power)
    inverse = lax.rsqrt(distsq + product * damping)
    cubed = SOLVENT_FACTOR * (atoms[3] * others[3]) * inverse * inverse * inverse
    radial = jnp.sum(0.5 * cubed * damping * (1.0 + power) * others[6], axis=2)
    coulomb = weight * (atoms[3] * others[3]) * bare * bare * bare
    factor = cubed * (1.0 - 0.25 * damping) - coulomb
    return jnp.concatenate([radial[None], jnp.sum(factor[None] * displace, axis=3)])


def shared_chain(own, tile, ids):
    atoms, others, displace, distsq = split_pair(own, tile)
    inv_own = 1.0 / (distsq + atoms[4] * atoms[4])
    inv_other = 1.0 / (distsq + others[4] * others[4])
    factor = atoms[6] * others[5] * (inv_other * inv_other * inv_other)
    factor = factor + others[6] * atoms[5] * (inv_own * inv_own * inv_own)
    return jnp.sum(-4.0 * factor[None] * displace, axis=3)


def shared_conformation(type_radius, type_volume, packed, exclusions, axis):
    kinds = packed[:, 4].astype(jnp.int32)
    radius = type_radius[kinds]
    volume = type_volume[kinds]
    base = jnp.concatenate([packed[:, :4], radius[:, None], volume[:, None]], axis=1)
    length = packed.shape[2]
    ids = lax.axis_index(axis) * length + jnp.arange(length, dtype=jnp.int32)

    def gathered(block):
        return lax.all_gather(block, axis, axis=2, tiled=True)

    everyone = gathered(base)
    integral = shared_sum(shared_descreen, (base, ids, exclusions), everyone, 1)[0]
    saturation = jnp.tanh(radius * integral)
    born = 1.0 / (1.0 / radius - saturation / (radius + 0.09))
    slope = born * born * (1.0 - saturation * saturation) * radius / (radius + 0.09)
    with_born = jnp.concatenate([everyone, gathered(born[:, None])], axis=1)
    own_born = jnp.concatenate([base, born[:, None]], axis=1)
    second = shared_sum(shared_born, (own_born, ids, exclusions), with_born, 4)
    chained = second[0] * slope
    with_chain = jnp.concatenate([everyone, gathered(chained[:, None])], axis=1)
    own_chain = jnp.concatenate([base, chained[:, None]], axis=1)
    third = shared_sum(shared_chain, (own_chain, ids, exclusions), with_chain, 3)
    return jnp.concatenate([-(second[1:] + third), born[None]]).transpose(1, 0, 2)


def on_device(positions, charges, atom_types, exclusions, type_radius, type_volume):
    replicas, _, owned = positions.shape
    columns = lax.axis_size("col")
    devices = lax.axis_size("row") * columns
    if replicas == devices and devices * owned == SUBLANES * LANES:
        both = ("row", "col")
        packed = pack(positions, charges, atom_types, exclusions, type_radius, type_volume)
        recv = lax.all_to_all(packed.reshape(replicas, 2, LANES), both, split_axis=0, concat_axis=0, tiled=True)
        result = whole_conformation(recv.reshape(replicas * 2, LANES))
        back = lax.all_to_all(result.reshape(replicas, 1, LANES), both, split_axis=0, concat_axis=0, tiled=True)
        return unpack(back.reshape(replicas, LANES))
    shared = jnp.concatenate([charges, atom_types.astype(jnp.float32)])
    planes = [positions.reshape(replicas, 3 * owned), jnp.broadcast_to(shared[None], (replicas, 2 * owned))]
    local = replicas // columns
    recv = lax.all_to_all(jnp.concatenate(planes, axis=1), "col", split_axis=0, concat_axis=0, tiled=True)
    recv = recv.reshape(columns, local, 5, owned).transpose(1, 2, 0, 3).reshape(local, 5, columns * owned)
    result = shared_conformation(type_radius, type_volume, recv, exclusions, "row")
    result = result.reshape(local, 4, columns, owned).transpose(2, 0, 1, 3).reshape(replicas, 4 * owned)
    back = lax.all_to_all(result, "col", split_axis=0, concat_axis=0, tiled=True).reshape(replicas, 4, owned)
    return (back[:, :3], back[:, 3])


def solution(mesh):
    return jax.shard_map(
        on_device,
        mesh=mesh,
        in_specs=(
            P(None, None, ("row", "col")),
            P(("row", "col")),
            P(("row", "col")),
            P("row"),
            P(),
            P(),
        ),
        out_specs=(P(None, None, ("row", "col")), P(None, ("row", "col"))),
        check_vma=False,
    )
```

time: 364 us -> 34 us (0.09)
  waiting for transfers between devices: 183 us -> 0 us
  blocking collectives: 109 us -> 23.9 us
  other arithmetic: 46.1 us -> 0 us
  between operations: 14 us -> 0.64 us
  local copies, waits for them, and re-layouts: 10.2 us -> 0 us
  Pallas kernels: 0 us -> 9.2 us
    unnamed x6 -> x0, waiting for transfers between devices: 183 us -> none
    all_gather x6 -> x0, blocking collectives: 109 us -> none  [the longest x3 92.4 us: along_rows(): return lax.all_gather(packed, 'col', axis=1, tiled=True)]
    reduce_sum x29 -> x0, other arithmetic: 39.7 us -> none  [the longest x12 12.6 us: geometry(): distsq = jnp.sum(displace * displace, axis=0)]
    all_to_all x0 -> x2, blocking collectives: none -> 23.9 us  [the longest x1 14.5 us: on_device(): lax.all_to_all(packed.reshape(replicas, 2, LANES), both, split_axis=0, co...]
    pallas_call x0 -> x3, Pallas kernels: none -> 9.2 us  [the longest x1 6.13 us: whole_conformation(): pl.pallas_call(conformation_kernel, out_shape=jax.ShapeDtypeStruct((recv....]
    unnamed x21 -> x0, local copies, waits for them, and re-layouts: 6.37 us -> none
  transfers between devices with their start and end apart: 3 -> 0, of which waited for: 3 -> 0; matrix products, arithmetic and copies ran while one was open for 0% -> 0% of each run, Pallas kernels for 0% -> 0%
where the time goes in v1:
time: 34 us; the launch traced here: 33.8 us
  blocking collectives  23.9 us (70%)
  Pallas kernels  9.2 us (27%)
  between operations  0.64 us (2%)
    all_to_all x1, blocking collectives, on_device(): lax.all_to_all(packed.reshape(replicas, 2, LANES), both, split_axis=0, co...  14.5 us
    all_to_all x1, blocking collectives, on_device(): lax.all_to_all(result.reshape(replicas, 1, LANES), both, split_axis=0, co...  9.42 us
    pallas_call x1, Pallas kernels, whole_conformation(): pl.pallas_call(conformation_kernel, out_shape=jax.ShapeDtypeStruct((recv....  6.13 us
    pallas_call x1, Pallas kernels, pack(): pl.pallas_call(pack_kernel, out_shape=jax.ShapeDtypeStruct((replicas * 2,...  1.63 us
    pallas_call x1, Pallas kernels, unpack(): pl.pallas_call(unpack_kernel, out_shape=[jax.ShapeDtypeStruct(*forces), j...  1.44 us

profile of v1, /device:TPU:0, one launch (start us, length us, event | category | flops | bytes accessed | tf_op | source)
XLA Modules:
  0.0 33.8 jit_solution(14881198982238700963)
XLA Ops:
  0.6 1.6 %shard_map.77 = f32[64,128]{1,0:T(8,128)} custom-call(f32[3,32,32]{2,1,0:T(8,128)} %bitcast.17, f32[1,32]{1,0:T(1,128)} %bitcast.19, s32[1,32]{1,0:T(1,128)} %bitcast.20, s32[2,128]{1,0:T(2,128)} %bitcast.18, f32[1,32]{1,0:T(1,128)} %bitcast.21, f32[1,32]{1,0:T(1,128)} %bitcast.22), custom_call_target="tpu_custom_call" | custom-call | tf_op jit(solution)/shard_map/pallas_call | solution.py:71
  2.3 14.5 %all_to_all.10 = f32[32,2,128]{2,1,0:T(2,128)S(1)} all-to-all(f32[32,2,128]{2,1,0:T(2,128)} %bitcast.15), channel_id=1, replica_groups=mesh['row'=4,'col'=8] {'row','col'}, dimensions={0} | all-to-all | bytes 65536 | tf_op jit(solution)/shard_map/all_to_all | solution.py:372
  16.8 6.1 %shard_map.78 = f32[32,128]{1,0:T(8,128)S(1)} custom-call(f32[64,128]{1,0:T(8,128)S(1)} %bitcast.13), custom_call_target="tpu_custom_call" | custom-call | tf_op jit(solution)/shard_map/pallas_call | solution.py:236
  22.9 9.4 %all_to_all.11 = f32[32,1,128]{2,1,0:T(1,128)} all-to-all(f32[32,1,128]{2,1,0:T(1,128)S(1)} %bitcast.14), channel_id=1, replica_groups=mesh['row'=4,'col'=8] {'row','col'}, dimensions={0} | all-to-all | bytes 32768 | tf_op jit(solution)/shard_map/all_to_all | solution.py:374
  32.3 1.4 %shard_map.79 = (f32[3,32,32]{2,1,0:T(8,128)}, f32[32,32]{1,0:T(8,128)}) custom-call(f32[32,128]{1,0:T(8,128)} %bitcast.16), custom_call_target="tpu_custom_call" | custom-call | tf_op jit(solution)/shard_map/pallas_call | solution.py:274

commit v2 on v1

--- a/solution.py
+++ b/solution.py
@@ -15,7 +15,6 @@
 
 
 TURNS = 64
-TOGETHER = 21
 X, Y, Z, Q, RHO2, VOL, BORN, DECAY, QBORN, CHAIN = range(10)
 
 
@@ -70,7 +69,7 @@
     anywhere = pl.BlockSpec(memory_space=pl.ANY)
     return pl.pallas_call(
         pack_kernel,
-        out_shape=jax.ShapeDtypeStruct((replicas * 2, LANES), jnp.float32),
+        out_shape=pltpu.VMEM((replicas * 2, LANES), jnp.float32),
         in_specs=[anywhere] * 6,
         out_specs=pl.BlockSpec(memory_space=pltpu.VMEM),
         scratch_shapes=[
@@ -82,18 +81,23 @@
             pltpu.VMEM((1,) + type_volume.shape, jnp.float32),
             pltpu.SemaphoreType.DMA((6,)),
         ],
-        compiler_params=pltpu.CompilerParams(vmem_limit_bytes=60 * 1024 * 1024),
+        compiler_params=pltpu.CompilerParams(vmem_limit_bytes=4 * 1024 * 1024),
     )(
-        positions.transpose(1, 0, 2),
-        charges[None],
-        atom_types[None],
-        exclusions.reshape(lines, LANES),
-        type_radius[None],
-        type_volume[None],
+        *[
+            pltpu.with_memory_space_constraint(operand, pltpu.HBM)
+            for operand in (
+                positions.transpose(1, 0, 2),
+                charges[None],
+                atom_types[None],
+                exclusions.reshape(lines, LANES),
+                type_radius[None],
+                type_volume[None],
+            )
+        ]
     )
 
 
-def conformation_kernel(recv_ref, out_ref, turned, moved, shown, backs, pair_a, pair_b, pair_c, pair_d):
+def conformation_kernel(recv_ref, out_ref, turned, moved, backs, pair_a, pair_b, pair_c, pair_d):
     owners = out_ref.shape[0]
     per = owners // SUBLANES
     owned = LANES // per
@@ -108,9 +112,7 @@
     def keep(k, value, move=None):
         for drop in range(SUBLANES):
             turned[k, drop] = pltpu.roll(value, drop, 0) if drop else value
-        move = value if move is None else move
-        for turn in range(TURNS + 1):
-            moved[k, turn] = pltpu.roll(move, turn, 1) if turn else move
+        moved[k, 0] = value if move is None else move
 
     x, y, z, q, rho, vol, marks = [dense(k) for k in range(7)]
     for k, value in ((X, x), (Y, y), (Z, z), (RHO2, rho * rho), (VOL, vol)):
@@ -119,48 +121,46 @@
     one = jnp.ones(shape, jnp.float32)
 
     def sweep(pair, names, fields):
-        def block(first, turns, drops, stay, two_sided=range(SUBLANES)):
-            stayer = {drop: {k: turned[k, drop] for k in names} for drop in drops}
-            stay = [list(line) for line in stay]
-            for t in range(turns):
-                turn = first + t
-                mover = {k: moved[k, turn] for k in names}
-                back = None
-                for n, drop in enumerate(drops):
-                    to_mover, to_stayer = pair(mover, stayer[drop], turn, drop)
-                    stay[n] = [a + b for a, b in zip(stay[n], to_stayer)]
-                    if drop in two_sided:
-                        back = to_mover if back is None else [a + b for a, b in zip(back, to_mover)]
-                if back is not None:
-                    for k in range(fields):
-                        backs[k, drops[0] // half, turn] = back[k]
-            return stay
-
         total = [[zero] * 4 for _ in range(fields)]
+        edges = (0, TURNS)
         for part in range(2):
             drops = list(range(part * half, (part + 1) * half))
-            stay = [[zero] * fields for _ in drops]
-            for turn in (0, TURNS):
-                edge = drops if part == 0 else drops[:1]
-                stay[: len(edge)] = block(turn, 1, edge, stay[: len(edge)], two_sided=range(1, half))
-
-            def steps(i, state):
-                return block(i * TOGETHER + 1, TOGETHER, drops, state)
-
-            stay = lax.fori_loop(0, (TURNS - 1) // TOGETHER, steps, stay)
+            stayer = {drop: {k: turned[k, drop] for k in names} for drop in drops}
+            stay = {drop: [zero] * fields for drop in drops}
+            for turn in range(TURNS + 1):
+                if turn == 0:
+                    mover = {k: moved[k, 0] for k in names}
+                elif part == 0:
+                    mover = {k: pltpu.roll(moved[k, 0], turn, 1) for k in names}
+                    for k in names:
+                        moved[k, turn] = mover[k]
+                else:
+                    mover = {k: moved[k, turn] for k in names}
+                back = None
+                for drop in drops:
+                    if turn in edges and drop > half:
+                        continue
+                    to_mover, to_stayer = pair(mover, stayer[drop], turn, drop)
+                    stay[drop] = [a + b for a, b in zip(stay[drop], to_stayer)]
+                    if turn in edges and drop in (0, half):
+                        continue
+                    back = to_mover if back is None else [a + b for a, b in zip(back, to_mover)]
+                if part == 0 and turn not in edges:
+                    for k in range(fields):
+                        backs[k, turn] = back[k]
+                elif back is not None:
+                    for k in range(fields):
+                        value = back[k] if turn in edges else back[k] + backs[k, turn]
+                        value = pltpu.roll(value, LANES - turn, 1) if turn else value
+                        total[k][turn % 4] = total[k][turn % 4] + value
             for n, drop in enumerate(drops):
                 for k in range(fields):
-                    total[k][n] = total[k][n] + (pltpu.roll(stay[n][k], SUBLANES - drop, 0) if drop else stay[n][k])
-        for k in range(fields):
-            for turn in range(TURNS + 1):
-                back = backs[k, 0, turn]
-                if turn not in (0, TURNS):
-                    back = back + backs[k, 1, turn]
-                total[k][turn % 4] = total[k][turn % 4] + (pltpu.roll(back, LANES - turn, 1) if turn else back)
+                    value = pltpu.roll(stay[drop][k], SUBLANES - drop, 0) if drop else stay[drop][k]
+                    total[k][n] = total[k][n] + value
         return [(t[0] + t[1]) + (t[2] + t[3]) for t in total]
 
     def itself(turn, drop):
-        return isinstance(turn, int) and turn == 0 and drop == 0
+        return turn == 0 and drop == 0
 
     def descreen(mover, stayer, turn, drop):
         dx, dy, dz = [mover[k] - stayer[k] for k in (X, Y, Z)]
@@ -190,7 +190,8 @@
         power = distsq * (mover[DECAY] * stayer[DECAY])
         damping = jnp.exp2(power)
         effective = distsq + (mover[BORN] * stayer[BORN]) * damping
-        cubed = lax.rsqrt(effective) * pltpu.reciprocal(effective, approx=True)
+        inverse = lax.rsqrt(effective)
+        cubed = inverse * inverse * inverse
         pair_d[turn, drop] = cubed * (SOLVENT_FACTOR - (0.25 * SOLVENT_FACTOR) * damping)
         radial = cubed * (damping * (1.0 / math.log(2.0) - power))
         return [radial * stayer[QBORN]], [radial * mover[QBORN]]
@@ -201,22 +202,19 @@
     keep(Q, q)
     marks = marks.astype(jnp.int32)
     lane = lax.broadcasted_iota(jnp.int32, shape, 1)
-    for turn in range(1, TURNS):
-        if turn <= BAND:
-            marked = jnp.bitwise_and(jnp.right_shift(pltpu.roll(marks, turn, 1), turn - 1), 1) == 1
-            shown[turn, 0] = jnp.where(marked & (lane >= turn), 0.0, 1.0)
-            shown[turn, 1] = jnp.where(marked & (lane < turn), 0.0, 1.0)
-        else:
-            shown[turn, 0] = one
-            shown[turn, 1] = one
+
+    def hidden(turn, drop):
+        marked = jnp.bitwise_and(jnp.right_shift(pltpu.roll(marks, turn, 1), turn - 1), 1) == 1
+        return marked & (lane >= turn if drop == 0 else lane < turn)
 
     def force_terms(mover, stayer, turn, drop):
         if itself(turn, drop):
             return [zero] * 3, [zero] * 3
         distsq = pair_a[turn, drop]
-        bare = lax.rsqrt(distsq) * pltpu.reciprocal(distsq, approx=True)
-        if drop in (0, SUBLANES - 1) and not isinstance(turn, int):
-            bare = bare * shown[turn, min(drop, 1)]
+        bare = lax.rsqrt(distsq)
+        bare = bare * bare * bare
+        if drop in (0, SUBLANES - 1) and 1 <= turn <= BAND:
+            bare = jnp.where(hidden(turn, drop), 0.0, bare)
         chain = stayer[CHAIN] * pair_b[turn, drop] + mover[CHAIN] * pair_c[turn, drop]
         factor = chain + (bare - pair_d[turn, drop]) * (mover[Q] * stayer[Q])
         push = [factor * (mover[k] - stayer[k]) for k in (X, Y, Z)]
@@ -241,8 +239,7 @@
         scratch_shapes=[
             pltpu.VMEM((10, SUBLANES) + dense, jnp.float32),
             pltpu.VMEM((10, TURNS + 1) + dense, jnp.float32),
-            pltpu.VMEM((TURNS, 2) + dense, jnp.float32),
-            pltpu.VMEM((3, 2, TURNS + 1) + dense, jnp.float32),
+            pltpu.VMEM((3, TURNS + 1) + dense, jnp.float32),
             kept,
             kept,
             kept,
@@ -277,7 +274,8 @@
         in_specs=[pl.BlockSpec(memory_space=pltpu.VMEM)],
         out_specs=[anywhere, anywhere],
         scratch_shapes=[pltpu.VMEM(*forces), pltpu.VMEM(*born), pltpu.SemaphoreType.DMA((4,))],
-    )(back)
+        compiler_params=pltpu.CompilerParams(vmem_limit_bytes=4 * 1024 * 1024),
+    )(pltpu.with_memory_space_constraint(back, pltpu.VMEM))
     return (forces.transpose(1, 0, 2), born)
 
 

time: 34 us -> 30.8 us (0.906)
  Pallas kernels: 9.2 us -> 6.83 us
  blocking collectives: 23.9 us -> 23.1 us
    pallas_call x1, Pallas kernels: 6.13 us -> 5.08 us  [whole_conformation(): pl.pallas_call(conformation_kernel, out_shape=jax.ShapeDtypeStruct((recv....]
    pallas_call x1, Pallas kernels: 1.44 us -> 0.73 us  [unpack(): pl.pallas_call(unpack_kernel, out_shape=[jax.ShapeDtypeStruct(*forces), j...]
    all_to_all x1, blocking collectives: 9.42 us -> 8.8 us  [on_device(): lax.all_to_all(result.reshape(replicas, 1, LANES), both, split_axis=0, co...]
    pallas_call x1, Pallas kernels: 1.63 us -> 1.02 us  [pack(): pl.pallas_call(pack_kernel, out_shape=pltpu.VMEM((replicas * 2, LANES), j...]
where the time goes in v2:
time: 30.8 us; the launch traced here: 30.6 us
  blocking collectives  23.1 us (75%)
  Pallas kernels  6.83 us (22%)
  between operations  0.64 us (2%)
    all_to_all x1, blocking collectives, on_device(): lax.all_to_all(packed.reshape(replicas, 2, LANES), both, split_axis=0, co...  14.3 us
    all_to_all x1, blocking collectives, on_device(): lax.all_to_all(result.reshape(replicas, 1, LANES), both, split_axis=0, co...  8.8 us
    pallas_call x1, Pallas kernels, whole_conformation(): pl.pallas_call(conformation_kernel, out_shape=jax.ShapeDtypeStruct((recv....  5.08 us
    pallas_call x1, Pallas kernels, pack(): pl.pallas_call(pack_kernel, out_shape=pltpu.VMEM((replicas * 2, LANES), j...  1.02 us
    pallas_call x1, Pallas kernels, unpack(): pl.pallas_call(unpack_kernel, out_shape=[jax.ShapeDtypeStruct(*forces), j...  0.73 us

profile of v2, /device:TPU:0, one launch (start us, length us, event | category | flops | bytes accessed | tf_op | source)
XLA Modules:
  0.0 30.6 jit_solution(1937498753477901176)
XLA Ops:
  0.6 1.0 %shard_map.77 = f32[64,128]{1,0:T(8,128)S(1)} custom-call(f32[3,32,32]{2,1,0:T(8,128)} %bitcast.17, f32[1,32]{1,0:T(1,128)} %bitcast.19, s32[1,32]{1,0:T(1,128)} %bitcast.20, s32[2,128]{1,0:T(2,128)} %bitcast.18, f32[1,32]{1,0:T(1,128)} %bitcast.21, f32[1,32]{1,0:T(1,128)} %bitcast.22), custom_call_target="tpu_custom_call" | custom-call | tf_op jit(solution)/shard_map/pallas_call | solution.py:70
  1.7 14.3 %all_to_all.10 = f32[32,2,128]{2,1,0:T(2,128)S(1)} all-to-all(f32[32,2,128]{2,1,0:T(2,128)S(1)} %bitcast.14), channel_id=1, replica_groups=mesh['row'=4,'col'=8] {'row','col'}, dimensions={0} | all-to-all | bytes 65536 | tf_op jit(solution)/shard_map/all_to_all | solution.py:370
  15.9 5.1 %shard_map.78 = f32[32,128]{1,0:T(8,128)S(1)} custom-call(f32[64,128]{1,0:T(8,128)S(1)} %bitcast.13), custom_call_target="tpu_custom_call" | custom-call | tf_op jit(solution)/shard_map/pallas_call | solution.py:234
  21.0 8.8 %all_to_all.11 = f32[32,1,128]{2,1,0:T(1,128)S(1)} all-to-all(f32[32,1,128]{2,1,0:T(1,128)S(1)} %bitcast.15), channel_id=1, replica_groups=mesh['row'=4,'col'=8] {'row','col'}, dimensions={0} | all-to-all | bytes 32768 | tf_op jit(solution)/shard_map/all_to_all | solution.py:372
  29.8 0.7 %shard_map.79 = (f32[3,32,32]{2,1,0:T(8,128)}, f32[32,32]{1,0:T(8,128)}) custom-call(f32[32,128]{1,0:T(8,128)S(1)} %bitcast.16), custom_call_target="tpu_custom_call" | custom-call | tf_op jit(solution)/shard_map/pallas_call | solution.py:271

commit v3 on v2

--- a/solution.py
+++ b/solution.py
@@ -59,8 +59,11 @@
 
     first = [positions[0], positions[1], positions[2], everywhere(charges[...])]
     second = [everywhere(look_up(radius)), everywhere(look_up(volume)), everywhere(picked), jnp.zeros((replicas, owned), jnp.float32)]
-    out_ref[pl.ds(0, replicas, stride=2), :] = jnp.concatenate(first, axis=1)
-    out_ref[pl.ds(1, replicas, stride=2), :] = jnp.concatenate(second, axis=1)
+    rows, columns = lax.axis_size("row"), lax.axis_size("col")
+    for part, planes in enumerate((first, second)):
+        block = jnp.concatenate(planes, axis=1)
+        for r in range(rows):
+            out_ref[pl.ds(2 * r + part, columns, stride=2 * rows), :] = block[r * columns : (r + 1) * columns]
 
 
 def pack(positions, charges, atom_types, exclusions, type_radius, type_volume):
@@ -97,16 +100,21 @@
     )
 
 
-def conformation_kernel(recv_ref, out_ref, turned, moved, backs, pair_a, pair_b, pair_c, pair_d):
+def conformation_kernel(recv_ref, out_ref, staged, turned, moved, backs, pair_a, pair_b, pair_c, pair_d):
     owners = out_ref.shape[0]
     per = owners // SUBLANES
     owned = LANES // per
     shape = (SUBLANES, LANES)
     half = SUBLANES // 2
 
+    rows, columns = lax.axis_size("row"), lax.axis_size("col")
+    for part in range(2):
+        for r in range(rows):
+            staged[part, r * columns : (r + 1) * columns] = recv_ref[pl.ds(2 * r + part, columns, stride=2 * rows), :]
+
     def dense(k):
         part, first = k // per, k % per * owned
-        rows = [recv_ref[pl.ds(2 * j + part, SUBLANES, stride=2 * per), :] for j in range(per)]
+        rows = [staged[part, pl.ds(j, SUBLANES, stride=per), :] for j in range(per)]
         return jnp.concatenate([row[:, first : first + owned] for row in rows], axis=1)
 
     def keep(k, value, move=None):
@@ -222,9 +230,11 @@
 
     results = sweep(force_terms, (X, Y, Z, Q, CHAIN), 3) + [born]
     for j in range(per):
-        out_ref[pl.ds(j, SUBLANES, stride=per), :] = jnp.concatenate(
+        staged[0, pl.ds(j, SUBLANES, stride=per), :] = jnp.concatenate(
             [value[:, j * owned : (j + 1) * owned] for value in results], axis=1
         )
+    for r in range(rows):
+        out_ref[pl.ds(r, columns, stride=rows), :] = staged[0, r * columns : (r + 1) * columns]
 
 
 def whole_conformation(recv):
@@ -237,6 +247,7 @@
         in_specs=[vmem],
         out_specs=vmem,
         scratch_shapes=[
+            pltpu.VMEM((2, recv.shape[0] // 2, LANES), jnp.float32),
             pltpu.VMEM((10, SUBLANES) + dense, jnp.float32),
             pltpu.VMEM((10, TURNS + 1) + dense, jnp.float32),
             pltpu.VMEM((3, TURNS + 1) + dense, jnp.float32),
@@ -251,11 +262,18 @@
 
 def unpack_kernel(back_ref, forces_any, born_any, forces, born, sent):
     owned = born.shape[1]
-    born[...] = back_ref[:, 3 * owned : 4 * owned]
+    rows, columns = lax.axis_size("row"), lax.axis_size("col")
+    by_row = [back_ref[pl.ds(r, columns, stride=rows), :] for r in range(rows)]
+
+    def lay_out(target, plane):
+        for r in range(rows):
+            target[r * columns : (r + 1) * columns, :] = by_row[r][:, plane * owned : (plane + 1) * owned]
+
+    lay_out(born, 3)
     moves = [pltpu.make_async_copy(born, born_any, sent.at[3])]
     moves[0].start()
     for axis in range(3):
-        forces[axis] = back_ref[:, axis * owned : (axis + 1) * owned]
+        lay_out(forces.at[axis], axis)
         moves.append(pltpu.make_async_copy(forces.at[axis], forces_any.at[axis], sent.at[axis]))
         moves[-1].start()
     for move in moves:
@@ -365,7 +383,7 @@
     columns = lax.axis_size("col")
     devices = lax.axis_size("row") * columns
     if replicas == devices and devices * owned == SUBLANES * LANES:
-        both = ("row", "col")
+        both = ("col", "row")
         packed = pack(positions, charges, atom_types, exclusions, type_radius, type_volume)
         recv = lax.all_to_all(packed.reshape(replicas, 2, LANES), both, split_axis=0, concat_axis=0, tiled=True)
         result = whole_conformation(recv.reshape(replicas * 2, LANES))

time: 30.8 us -> 30.9 us (level)
  no operation moved by 1% of the time
where the time goes in v3:
time: 30.9 us; the launch traced here: 30.7 us
  blocking collectives  23.2 us (75%)
  Pallas kernels  6.84 us (22%)
  between operations  0.64 us (2%)
    all_to_all x1, blocking collectives, on_device(): lax.all_to_all(packed.reshape(replicas, 2, LANES), both, split_axis=0, co...  14.4 us
    all_to_all x1, blocking collectives, on_device(): lax.all_to_all(result.reshape(replicas, 1, LANES), both, split_axis=0, co...  8.84 us
    pallas_call x1, Pallas kernels, whole_conformation(): pl.pallas_call(conformation_kernel, out_shape=jax.ShapeDtypeStruct((recv....  5.1 us
    pallas_call x1, Pallas kernels, pack(): pl.pallas_call(pack_kernel, out_shape=pltpu.VMEM((replicas * 2, LANES), j...  1.02 us
    pallas_call x1, Pallas kernels, unpack(): pl.pallas_call(unpack_kernel, out_shape=[jax.ShapeDtypeStruct(*forces), j...  0.73 us

profile of v3, /device:TPU:0, one launch (start us, length us, event | category | flops | bytes accessed | tf_op | source)
XLA Modules:
  0.0 30.7 jit_solution(1872161766109534448)
XLA Ops:
  0.6 1.0 %shard_map.77 = f32[64,128]{1,0:T(8,128)S(1)} custom-call(f32[3,32,32]{2,1,0:T(8,128)} %bitcast.17, f32[1,32]{1,0:T(1,128)} %bitcast.19, s32[1,32]{1,0:T(1,128)} %bitcast.20, s32[2,128]{1,0:T(2,128)} %bitcast.18, f32[1,32]{1,0:T(1,128)} %bitcast.21, f32[1,32]{1,0:T(1,128)} %bitcast.22), custom_call_target="tpu_custom_call" | custom-call | tf_op jit(solution)/shard_map/pallas_call | solution.py:73
  1.7 14.4 %all_to_all.10 = f32[32,2,128]{2,1,0:T(2,128)S(1)} all-to-all(f32[32,2,128]{2,1,0:T(2,128)S(1)} %bitcast.14), channel_id=1, replica_groups=mesh['row'=4,'col'=8] {'col','row'}, dimensions={0} | all-to-all | bytes 65536 | tf_op jit(solution)/shard_map/all_to_all | solution.py:388
  16.0 5.1 %shard_map.78 = f32[32,128]{1,0:T(8,128)S(1)} custom-call(f32[64,128]{1,0:T(8,128)S(1)} %bitcast.13), custom_call_target="tpu_custom_call" | custom-call | tf_op jit(solution)/shard_map/pallas_call | solution.py:244
  21.1 8.8 %all_to_all.11 = f32[32,1,128]{2,1,0:T(1,128)S(1)} all-to-all(f32[32,1,128]{2,1,0:T(1,128)S(1)} %bitcast.15), channel_id=1, replica_groups=mesh['row'=4,'col'=8] {'col','row'}, dimensions={0} | all-to-all | bytes 32768 | tf_op jit(solution)/shard_map/all_to_all | solution.py:390
  30.0 0.7 %shard_map.79 = (f32[3,32,32]{2,1,0:T(8,128)}, f32[32,32]{1,0:T(8,128)}) custom-call(f32[32,128]{1,0:T(8,128)S(1)} %bitcast.16), custom_call_target="tpu_custom_call" | custom-call | tf_op jit(solution)/shard_map/pallas_call | solution.py:289

commit v4 on v2

--- a/solution.py
+++ b/solution.py
@@ -97,7 +97,7 @@
     )
 
 
-def conformation_kernel(recv_ref, out_ref, turned, moved, backs, pair_a, pair_b, pair_c, pair_d):
+def conformation_kernel(recv_ref, out_ref, turned, moved, backs, pair_a, pair_b, pair_c, pair_d, pair_e):
     owners = out_ref.shape[0]
     per = owners // SUBLANES
     owned = LANES // per
@@ -125,22 +125,22 @@
         edges = (0, TURNS)
         for part in range(2):
             drops = list(range(part * half, (part + 1) * half))
-            stayer = {drop: {k: turned[k, drop] for k in names} for drop in drops}
             stay = {drop: [zero] * fields for drop in drops}
             for turn in range(TURNS + 1):
                 if turn == 0:
                     mover = {k: moved[k, 0] for k in names}
                 elif part == 0:
-                    mover = {k: pltpu.roll(moved[k, 0], turn, 1) for k in names}
                     for k in names:
-                        moved[k, turn] = mover[k]
+                        moved[k, turn] = pltpu.roll(moved[k, 0], turn, 1)
+                    mover = {k: moved[k, turn] for k in names}
                 else:
                     mover = {k: moved[k, turn] for k in names}
                 back = None
                 for drop in drops:
                     if turn in edges and drop > half:
                         continue
-                    to_mover, to_stayer = pair(mover, stayer[drop], turn, drop)
+                    stayer = {k: turned[k, drop] for k in names}
+                    to_mover, to_stayer = pair(mover, stayer, turn, drop)
                     stay[drop] = [a + b for a, b in zip(stay[drop], to_stayer)]
                     if turn in edges and drop in (0, half):
                         continue
@@ -177,13 +177,34 @@
         return [from_stayer], [from_mover]
 
     (integral,) = sweep(descreen, (X, Y, Z, RHO2, VOL), 1)
+    inv_rho = pltpu.reciprocal(rho, approx=True)
+    inv_shell = pltpu.reciprocal(rho + 0.09, approx=True)
     saturation = jnp.tanh(rho * integral)
-    born = 1.0 / (1.0 / rho - saturation / (rho + 0.09))
-    slope = born * born * (1.0 - saturation * saturation) * rho / (rho + 0.09)
-    decay = (math.sqrt(math.log2(math.e)) / 2.0) / born
+    inv_born = inv_rho - saturation * inv_shell
+    born = pltpu.reciprocal(inv_born, approx=True)
+    decay = (math.sqrt(math.log2(math.e)) / 2.0) * inv_born
     keep(BORN, born)
     keep(DECAY, decay, -decay)
     keep(QBORN, q * born)
+    slope = born * born * (1.0 - saturation * saturation) * (rho * inv_shell)
+    to_chain = (2.0 * SOLVENT_FACTOR * math.log(2.0)) * q * slope
+    marks = marks.astype(jnp.int32)
+    lane = lax.broadcasted_iota(jnp.int32, shape, 1)
+
+    def bare_coulomb(part):
+        for turn in range(TURNS + 1):
+            if 1 <= turn <= BAND:
+                marked = jnp.bitwise_and(jnp.right_shift(pltpu.roll(marks, turn, 1), turn - 1), 1) == 1
+            for drop in range(part * half, (part + 1) * half):
+                if itself(turn, drop) or (turn in (0, TURNS) and drop > half):
+                    continue
+                bare = lax.rsqrt(pair_a[turn, drop])
+                bare = bare * bare * bare
+                if 1 <= turn <= BAND and drop in (0, SUBLANES - 1):
+                    bare = jnp.where(marked & (lane >= turn if drop == 0 else lane < turn), 0.0, bare)
+                pair_e[turn, drop] = bare
+
+    bare_coulomb(0)
 
     def born_terms(mover, stayer, turn, drop):
         distsq = pair_a[turn, drop]
@@ -197,26 +218,15 @@
         return [radial * stayer[QBORN]], [radial * mover[QBORN]]
 
     (radial,) = sweep(born_terms, (BORN, DECAY, QBORN), 1)
-    chained = (0.5 * SOLVENT_FACTOR * math.log(2.0)) * q * radial * slope
-    keep(CHAIN, 4.0 * chained)
+    keep(CHAIN, radial * to_chain)
     keep(Q, q)
-    marks = marks.astype(jnp.int32)
-    lane = lax.broadcasted_iota(jnp.int32, shape, 1)
-
-    def hidden(turn, drop):
-        marked = jnp.bitwise_and(jnp.right_shift(pltpu.roll(marks, turn, 1), turn - 1), 1) == 1
-        return marked & (lane >= turn if drop == 0 else lane < turn)
+    bare_coulomb(1)
 
     def force_terms(mover, stayer, turn, drop):
         if itself(turn, drop):
             return [zero] * 3, [zero] * 3
-        distsq = pair_a[turn, drop]
-        bare = lax.rsqrt(distsq)
-        bare = bare * bare * bare
-        if drop in (0, SUBLANES - 1) and 1 <= turn <= BAND:
-            bare = jnp.where(hidden(turn, drop), 0.0, bare)
         chain = stayer[CHAIN] * pair_b[turn, drop] + mover[CHAIN] * pair_c[turn, drop]
-        factor = chain + (bare - pair_d[turn, drop]) * (mover[Q] * stayer[Q])
+        factor = chain + (pair_e[turn, drop] - pair_d[turn, drop]) * (mover[Q] * stayer[Q])
         push = [factor * (mover[k] - stayer[k]) for k in (X, Y, Z)]
         return push, [-p for p in push]
 
@@ -240,6 +250,7 @@
             pltpu.VMEM((10, SUBLANES) + dense, jnp.float32),
             pltpu.VMEM((10, TURNS + 1) + dense, jnp.float32),
             pltpu.VMEM((3, TURNS + 1) + dense, jnp.float32),
+            kept,
             kept,
             kept,
             kept,

time: 30.8 us -> 30.8 us (level)
  no operation moved by 1% of the time
where the time goes in v4:
time: 30.8 us; the launch traced here: 30.6 us
  blocking collectives  23.1 us (75%)
  Pallas kernels  6.85 us (22%)
  between operations  0.64 us (2%)
    all_to_all x1, blocking collectives, on_device(): lax.all_to_all(packed.reshape(replicas, 2, LANES), both, split_axis=0, co...  14.3 us
    all_to_all x1, blocking collectives, on_device(): lax.all_to_all(result.reshape(replicas, 1, LANES), both, split_axis=0, co...  8.81 us
    pallas_call x1, Pallas kernels, whole_conformation(): pl.pallas_call(conformation_kernel, out_shape=jax.ShapeDtypeStruct((recv....  5.11 us
    pallas_call x1, Pallas kernels, pack(): pl.pallas_call(pack_kernel, out_shape=pltpu.VMEM((replicas * 2, LANES), j...  1.02 us
    pallas_call x1, Pallas kernels, unpack(): pl.pallas_call(unpack_kernel, out_shape=[jax.ShapeDtypeStruct(*forces), j...  0.73 us

profile of v4, /device:TPU:0, one launch (start us, length us, event | category | flops | bytes accessed | tf_op | source)
XLA Modules:
  0.0 30.6 jit_solution(10187989957060475388)
XLA Ops:
  0.6 1.0 %shard_map.77 = f32[64,128]{1,0:T(8,128)S(1)} custom-call(f32[3,32,32]{2,1,0:T(8,128)} %bitcast.17, f32[1,32]{1,0:T(1,128)} %bitcast.19, s32[1,32]{1,0:T(1,128)} %bitcast.20, s32[2,128]{1,0:T(2,128)} %bitcast.18, f32[1,32]{1,0:T(1,128)} %bitcast.21, f32[1,32]{1,0:T(1,128)} %bitcast.22), custom_call_target="tpu_custom_call" | custom-call | tf_op jit(solution)/shard_map/pallas_call | solution.py:70
  1.7 14.3 %all_to_all.10 = f32[32,2,128]{2,1,0:T(2,128)S(1)} all-to-all(f32[32,2,128]{2,1,0:T(2,128)S(1)} %bitcast.14), channel_id=1, replica_groups=mesh['row'=4,'col'=8] {'row','col'}, dimensions={0} | all-to-all | bytes 65536 | tf_op jit(solution)/shard_map/all_to_all | solution.py:381
  15.9 5.1 %shard_map.78 = f32[32,128]{1,0:T(8,128)S(1)} custom-call(f32[64,128]{1,0:T(8,128)S(1)} %bitcast.13), custom_call_target="tpu_custom_call" | custom-call | tf_op jit(solution)/shard_map/pallas_call | solution.py:244
  21.1 8.8 %all_to_all.11 = f32[32,1,128]{2,1,0:T(1,128)S(1)} all-to-all(f32[32,1,128]{2,1,0:T(1,128)S(1)} %bitcast.15), channel_id=1, replica_groups=mesh['row'=4,'col'=8] {'row','col'}, dimensions={0} | all-to-all | bytes 32768 | tf_op jit(solution)/shard_map/all_to_all | solution.py:383
  29.9 0.7 %shard_map.79 = (f32[3,32,32]{2,1,0:T(8,128)}, f32[32,32]{1,0:T(8,128)}) custom-call(f32[32,128]{1,0:T(8,128)S(1)} %bitcast.16), custom_call_target="tpu_custom_call" | custom-call | tf_op jit(solution)/shard_map/pallas_call | solution.py:282

commit v5 on v4

--- a/solution.py
+++ b/solution.py
@@ -103,6 +103,10 @@
     owned = LANES // per
     shape = (SUBLANES, LANES)
     half = SUBLANES // 2
+    place = lax.axis_index("col")
+
+    def seen(ref, n):
+        return ref.at[pl.ds(lax.shift_right_logical(place, 16 + n), ref.shape[0])]
 
     def dense(k):
         part, first = k // per, k % per * owned
@@ -123,6 +127,7 @@
     def sweep(pair, names, fields):
         total = [[zero] * 4 for _ in range(fields)]
         edges = (0, TURNS)
+        moved_later, backs_later = seen(moved, 0), seen(backs, 0)
         for part in range(2):
             drops = list(range(part * half, (part + 1) * half))
             stay = {drop: [zero] * fields for drop in drops}
@@ -130,11 +135,11 @@
                 if turn == 0:
                     mover = {k: moved[k, 0] for k in names}
                 elif part == 0:
+                    mover = {k: pltpu.roll(moved[k, 0], turn, 1) for k in names}
                     for k in names:
-                        moved[k, turn] = pltpu.roll(moved[k, 0], turn, 1)
-                    mover = {k: moved[k, turn] for k in names}
+                        moved[k, turn] = mover[k]
                 else:
-                    mover = {k: moved[k, turn] for k in names}
+                    mover = {k: moved_later[k, turn] for k in names}
                 back = None
                 for drop in drops:
                     if turn in edges and drop > half:
@@ -150,7 +155,7 @@
                         backs[k, turn] = back[k]
                 elif back is not None:
                     for k in range(fields):
-                        value = back[k] if turn in edges else back[k] + backs[k, turn]
+                        value = back[k] if turn in edges else back[k] + backs_later[k, turn]
                         value = pltpu.roll(value, LANES - turn, 1) if turn else value
                         total[k][turn % 4] = total[k][turn % 4] + value
             for n, drop in enumerate(drops):
@@ -192,13 +197,14 @@
     lane = lax.broadcasted_iota(jnp.int32, shape, 1)
 
     def bare_coulomb(part):
+        distances = seen(pair_a, 1 + part)
         for turn in range(TURNS + 1):
             if 1 <= turn <= BAND:
                 marked = jnp.bitwise_and(jnp.right_shift(pltpu.roll(marks, turn, 1), turn - 1), 1) == 1
             for drop in range(part * half, (part + 1) * half):
                 if itself(turn, drop) or (turn in (0, TURNS) and drop > half):
                     continue
-                bare = lax.rsqrt(pair_a[turn, drop])
+                bare = lax.rsqrt(distances[turn, drop])
                 bare = bare * bare * bare
                 if 1 <= turn <= BAND and drop in (0, SUBLANES - 1):
                     bare = jnp.where(marked & (lane >= turn if drop == 0 else lane < turn), 0.0, bare)
@@ -206,8 +212,10 @@
 
     bare_coulomb(0)
 
+    distances = seen(pair_a, 3)
+
     def born_terms(mover, stayer, turn, drop):
-        distsq = pair_a[turn, drop]
+        distsq = distances[turn, drop]
         power = distsq * (mover[DECAY] * stayer[DECAY])
         damping = jnp.exp2(power)
         effective = distsq + (mover[BORN] * stayer[BORN]) * damping
@@ -222,11 +230,13 @@
     keep(Q, q)
     bare_coulomb(1)
 
+    kept_b, kept_c, kept_d, kept_e = [seen(ref, 4) for ref in (pair_b, pair_c, pair_d, pair_e)]
+
     def force_terms(mover, stayer, turn, drop):
         if itself(turn, drop):
             return [zero] * 3, [zero] * 3
-        chain = stayer[CHAIN] * pair_b[turn, drop] + mover[CHAIN] * pair_c[turn, drop]
-        factor = chain + (pair_e[turn, drop] - pair_d[turn, drop]) * (mover[Q] * stayer[Q])
+        chain = stayer[CHAIN] * kept_b[turn, drop] + mover[CHAIN] * kept_c[turn, drop]
+        factor = chain + (kept_e[turn, drop] - kept_d[turn, drop]) * (mover[Q] * stayer[Q])
         push = [factor * (mover[k] - stayer[k]) for k in (X, Y, Z)]
         return push, [-p for p in push]
 

time: 30.8 us -> 30.7 us (level)
  no operation moved by 1% of the time
where the time goes in v5:
time: 30.7 us; the launch traced here: 30.5 us
  blocking collectives  23.1 us (75%)
  Pallas kernels  6.71 us (22%)
  between operations  0.65 us (2%)
    all_to_all x1, blocking collectives, on_device(): lax.all_to_all(packed.reshape(replicas, 2, LANES), both, split_axis=0, co...  14.3 us
    all_to_all x1, blocking collectives, on_device(): lax.all_to_all(result.reshape(replicas, 1, LANES), both, split_axis=0, co...  8.81 us
    pallas_call x1, Pallas kernels, whole_conformation(): pl.pallas_call(conformation_kernel, out_shape=jax.ShapeDtypeStruct((recv....  4.97 us
    pallas_call x1, Pallas kernels, pack(): pl.pallas_call(pack_kernel, out_shape=pltpu.VMEM((replicas * 2, LANES), j...  1.02 us
    pallas_call x1, Pallas kernels, unpack(): pl.pallas_call(unpack_kernel, out_shape=[jax.ShapeDtypeStruct(*forces), j...  0.73 us

profile of v5, /device:TPU:0, one launch (start us, length us, event | category | flops | bytes accessed | tf_op | source)
XLA Modules:
  0.0 30.5 jit_solution(382916365138998568)
XLA Ops:
  0.6 1.0 %shard_map.77 = f32[64,128]{1,0:T(8,128)S(1)} custom-call(f32[3,32,32]{2,1,0:T(8,128)} %bitcast.17, f32[1,32]{1,0:T(1,128)} %bitcast.19, s32[1,32]{1,0:T(1,128)} %bitcast.20, s32[2,128]{1,0:T(2,128)} %bitcast.18, f32[1,32]{1,0:T(1,128)} %bitcast.21, f32[1,32]{1,0:T(1,128)} %bitcast.22), custom_call_target="tpu_custom_call" | custom-call | tf_op jit(solution)/shard_map/pallas_call | solution.py:70
  1.7 14.3 %all_to_all.10 = f32[32,2,128]{2,1,0:T(2,128)S(1)} all-to-all(f32[32,2,128]{2,1,0:T(2,128)S(1)} %bitcast.14), channel_id=1, replica_groups=mesh['row'=4,'col'=8] {'row','col'}, dimensions={0} | all-to-all | bytes 65536 | tf_op jit(solution)/shard_map/all_to_all | solution.py:391
  15.9 5.0 %shard_map.78 = f32[32,128]{1,0:T(8,128)S(1)} custom-call(f32[64,128]{1,0:T(8,128)S(1)} %bitcast.13), custom_call_target="tpu_custom_call" | custom-call | tf_op jit(solution)/shard_map/pallas_call | solution.py:254
  20.9 8.8 %all_to_all.11 = f32[32,1,128]{2,1,0:T(1,128)S(1)} all-to-all(f32[32,1,128]{2,1,0:T(1,128)S(1)} %bitcast.15), channel_id=1, replica_groups=mesh['row'=4,'col'=8] {'row','col'}, dimensions={0} | all-to-all | bytes 32768 | tf_op jit(solution)/shard_map/all_to_all | solution.py:393
  29.7 0.7 %shard_map.79 = (f32[3,32,32]{2,1,0:T(8,128)}, f32[32,32]{1,0:T(8,128)}) custom-call(f32[32,128]{1,0:T(8,128)S(1)} %bitcast.16), custom_call_target="tpu_custom_call" | custom-call | tf_op jit(solution)/shard_map/pallas_call | solution.py:292

commit v6 on v5

--- a/solution.py
+++ b/solution.py
@@ -15,6 +15,7 @@
 
 
 TURNS = 64
+AHEAD = 5
 X, Y, Z, Q, RHO2, VOL, BORN, DECAY, QBORN, CHAIN = range(10)
 
 
@@ -130,16 +131,15 @@
         moved_later, backs_later = seen(moved, 0), seen(backs, 0)
         for part in range(2):
             drops = list(range(part * half, (part + 1) * half))
+            base = {k: moved[k, 0] for k in names}
             stay = {drop: [zero] * fields for drop in drops}
             for turn in range(TURNS + 1):
-                if turn == 0:
-                    mover = {k: moved[k, 0] for k in names}
-                elif part == 0:
-                    mover = {k: pltpu.roll(moved[k, 0], turn, 1) for k in names}
-                    for k in names:
-                        moved[k, turn] = mover[k]
-                else:
-                    mover = {k: moved_later[k, turn] for k in names}
+                if part == 0:
+                    for ahead in range(1, AHEAD + 1) if turn == 0 else [turn + AHEAD]:
+                        if ahead <= TURNS:
+                            for k in names:
+                                moved[k, ahead] = pltpu.roll(base[k], ahead, 1)
+                mover = {k: moved_later[k, turn] for k in names} if turn else base
                 back = None
                 for drop in drops:
                     if turn in edges and drop > half:

time: 30.7 us -> 31.7 us (1.033)
  Pallas kernels: 6.71 us -> 7.71 us
    pallas_call x1, Pallas kernels: 4.97 us -> 5.97 us  [whole_conformation(): pl.pallas_call(conformation_kernel, out_shape=jax.ShapeDtypeStruct((recv....]
where the time goes in v6:
time: 31.7 us; the launch traced here: 31.5 us
  blocking collectives  23.1 us (73%)
  Pallas kernels  7.71 us (24%)
  between operations  0.65 us (2%)
    all_to_all x1, blocking collectives, on_device(): lax.all_to_all(packed.reshape(replicas, 2, LANES), both, split_axis=0, co...  14.3 us
    all_to_all x1, blocking collectives, on_device(): lax.all_to_all(result.reshape(replicas, 1, LANES), both, split_axis=0, co...  8.81 us
    pallas_call x1, Pallas kernels, whole_conformation(): pl.pallas_call(conformation_kernel, out_shape=jax.ShapeDtypeStruct((recv....  5.97 us
    pallas_call x1, Pallas kernels, pack(): pl.pallas_call(pack_kernel, out_shape=pltpu.VMEM((replicas * 2, LANES), j...  1.02 us
    pallas_call x1, Pallas kernels, unpack(): pl.pallas_call(unpack_kernel, out_shape=[jax.ShapeDtypeStruct(*forces), j...  0.73 us

profile of v6, /device:TPU:0, one launch (start us, length us, event | category | flops | bytes accessed | tf_op | source)
XLA Modules:
  0.0 31.5 jit_solution(17645962661968289782)
XLA Ops:
  0.6 1.0 %shard_map.77 = f32[64,128]{1,0:T(8,128)S(1)} custom-call(f32[3,32,32]{2,1,0:T(8,128)} %bitcast.17, f32[1,32]{1,0:T(1,128)} %bitcast.19, s32[1,32]{1,0:T(1,128)} %bitcast.20, s32[2,128]{1,0:T(2,128)} %bitcast.18, f32[1,32]{1,0:T(1,128)} %bitcast.21, f32[1,32]{1,0:T(1,128)} %bitcast.22), custom_call_target="tpu_custom_call" | custom-call | tf_op jit(solution)/shard_map/pallas_call | solution.py:71
  1.7 14.3 %all_to_all.10 = f32[32,2,128]{2,1,0:T(2,128)S(1)} all-to-all(f32[32,2,128]{2,1,0:T(2,128)S(1)} %bitcast.14), channel_id=1, replica_groups=mesh['row'=4,'col'=8] {'row','col'}, dimensions={0} | all-to-all | bytes 65536 | tf_op jit(solution)/shard_map/all_to_all | solution.py:391
  15.9 6.0 %shard_map.78 = f32[32,128]{1,0:T(8,128)S(1)} custom-call(f32[64,128]{1,0:T(8,128)S(1)} %bitcast.13), custom_call_target="tpu_custom_call" | custom-call | tf_op jit(solution)/shard_map/pallas_call | solution.py:254
  21.9 8.8 %all_to_all.11 = f32[32,1,128]{2,1,0:T(1,128)S(1)} all-to-all(f32[32,1,128]{2,1,0:T(1,128)S(1)} %bitcast.15), channel_id=1, replica_groups=mesh['row'=4,'col'=8] {'row','col'}, dimensions={0} | all-to-all | bytes 32768 | tf_op jit(solution)/shard_map/all_to_all | solution.py:393
  30.7 0.7 %shard_map.79 = (f32[3,32,32]{2,1,0:T(8,128)}, f32[32,32]{1,0:T(8,128)}) custom-call(f32[32,128]{1,0:T(8,128)S(1)} %bitcast.16), custom_call_target="tpu_custom_call" | custom-call | tf_op jit(solution)/shard_map/pallas_call | solution.py:292

commit v7 on v5

--- a/solution.py
+++ b/solution.py
@@ -33,7 +33,7 @@
     ):
         moves.append(pltpu.make_async_copy(source, target, arrived.at[n]))
         moves[-1].start()
-    for move in moves:
+    for move in moves[1:]:
         move.wait()
     replicas, owned = positions.shape[1:]
 
@@ -57,10 +57,13 @@
     def everywhere(row):
         return jnp.broadcast_to(row, (replicas, owned))
 
-    first = [positions[0], positions[1], positions[2], everywhere(charges[...])]
-    second = [everywhere(look_up(radius)), everywhere(look_up(volume)), everywhere(picked), jnp.zeros((replicas, owned), jnp.float32)]
+    second = [everywhere(look_up(radius)), everywhere(look_up(volume)), everywhere(picked)]
+    second.append(jnp.zeros((replicas, owned), jnp.float32))
+    out_ref[pl.ds(1, replicas, stride=2), :] = jnp.concatenate(second, axis=1)
+    charge = everywhere(charges[...])
+    moves[0].wait()
+    first = [positions[0], positions[1], positions[2], charge]
     out_ref[pl.ds(0, replicas, stride=2), :] = jnp.concatenate(first, axis=1)
-    out_ref[pl.ds(1, replicas, stride=2), :] = jnp.concatenate(second, axis=1)
 
 
 def pack(positions, charges, atom_types, exclusions, type_radius, type_volume):
@@ -97,7 +100,7 @@
     )
 
 
-def conformation_kernel(recv_ref, out_ref, turned, moved, backs, pair_a, pair_b, pair_c, pair_d, pair_e):
+def conformation_kernel(recv_ref, out_ref, turned, moved, backs, pair_a, pair_b, pair_c, pair_d):
     owners = out_ref.shape[0]
     per = owners // SUBLANES
     owned = LANES // per
@@ -196,21 +199,9 @@
     marks = marks.astype(jnp.int32)
     lane = lax.broadcasted_iota(jnp.int32, shape, 1)
 
-    def bare_coulomb(part):
-        distances = seen(pair_a, 1 + part)
-        for turn in range(TURNS + 1):
-            if 1 <= turn <= BAND:
-                marked = jnp.bitwise_and(jnp.right_shift(pltpu.roll(marks, turn, 1), turn - 1), 1) == 1
-            for drop in range(part * half, (part + 1) * half):
-                if itself(turn, drop) or (turn in (0, TURNS) and drop > half):
-                    continue
-                bare = lax.rsqrt(distances[turn, drop])
-                bare = bare * bare * bare
-                if 1 <= turn <= BAND and drop in (0, SUBLANES - 1):
-                    bare = jnp.where(marked & (lane >= turn if drop == 0 else lane < turn), 0.0, bare)
-                pair_e[turn, drop] = bare
-
-    bare_coulomb(0)
+    def hidden(turn, drop):
+        marked = jnp.bitwise_and(jnp.right_shift(pltpu.roll(marks, turn, 1), turn - 1), 1) == 1
+        return marked & (lane >= turn if drop == 0 else lane < turn)
 
     distances = seen(pair_a, 3)
 
@@ -228,15 +219,18 @@
     (radial,) = sweep(born_terms, (BORN, DECAY, QBORN), 1)
     keep(CHAIN, radial * to_chain)
     keep(Q, q)
-    bare_coulomb(1)
-
-    kept_b, kept_c, kept_d, kept_e = [seen(ref, 4) for ref in (pair_b, pair_c, pair_d, pair_e)]
+
+    kept_a, kept_b, kept_c, kept_d = [seen(ref, 4) for ref in (pair_a, pair_b, pair_c, pair_d)]
 
     def force_terms(mover, stayer, turn, drop):
         if itself(turn, drop):
             return [zero] * 3, [zero] * 3
         chain = stayer[CHAIN] * kept_b[turn, drop] + mover[CHAIN] * kept_c[turn, drop]
-        factor = chain + (kept_e[turn, drop] - kept_d[turn, drop]) * (mover[Q] * stayer[Q])
+        bare = lax.rsqrt(kept_a[turn, drop])
+        bare = bare * bare * bare
+        if drop in (0, SUBLANES - 1) and 1 <= turn <= BAND:
+            bare = jnp.where(hidden(turn, drop), 0.0, bare)
+        factor = chain + (bare - kept_d[turn, drop]) * (mover[Q] * stayer[Q])
         push = [factor * (mover[k] - stayer[k]) for k in (X, Y, Z)]
         return push, [-p for p in push]
 
@@ -260,7 +254,6 @@
             pltpu.VMEM((10, SUBLANES) + dense, jnp.float32),
             pltpu.VMEM((10, TURNS + 1) + dense, jnp.float32),
             pltpu.VMEM((3, TURNS + 1) + dense, jnp.float32),
-            kept,
             kept,
             kept,
             kept,

time: 30.7 us -> 30.8 us (level)
  no operation moved by 1% of the time
where the time goes in v7:
time: 30.8 us; the launch traced here: 30.6 us
  blocking collectives  23.1 us (75%)
  Pallas kernels  6.81 us (22%)
  between operations  0.65 us (2%)
    all_to_all x1, blocking collectives, on_device(): lax.all_to_all(packed.reshape(replicas, 2, LANES), both, split_axis=0, co...  14.3 us
    all_to_all x1, blocking collectives, on_device(): lax.all_to_all(result.reshape(replicas, 1, LANES), both, split_axis=0, co...  8.81 us
    pallas_call x1, Pallas kernels, whole_conformation(): pl.pallas_call(conformation_kernel, out_shape=jax.ShapeDtypeStruct((recv....  5.05 us
    pallas_call x1, Pallas kernels, pack(): pl.pallas_call(pack_kernel, out_shape=pltpu.VMEM((replicas * 2, LANES), j...  1.03 us
    pallas_call x1, Pallas kernels, unpack(): pl.pallas_call(unpack_kernel, out_shape=[jax.ShapeDtypeStruct(*forces), j...  0.73 us

profile of v7, /device:TPU:0, one launch (start us, length us, event | category | flops | bytes accessed | tf_op | source)
XLA Modules:
  0.0 30.6 jit_solution(14807728683498832930)
XLA Ops:
  0.6 1.0 %shard_map.77 = f32[64,128]{1,0:T(8,128)S(1)} custom-call(f32[3,32,32]{2,1,0:T(8,128)} %bitcast.17, f32[1,32]{1,0:T(1,128)} %bitcast.19, s32[1,32]{1,0:T(1,128)} %bitcast.20, s32[2,128]{1,0:T(2,128)} %bitcast.18, f32[1,32]{1,0:T(1,128)} %bitcast.21, f32[1,32]{1,0:T(1,128)} %bitcast.22), custom_call_target="tpu_custom_call" | custom-call | tf_op jit(solution)/shard_map/pallas_call | solution.py:73
  1.7 14.3 %all_to_all.10 = f32[32,2,128]{2,1,0:T(2,128)S(1)} all-to-all(f32[32,2,128]{2,1,0:T(2,128)S(1)} %bitcast.14), channel_id=1, replica_groups=mesh['row'=4,'col'=8] {'row','col'}, dimensions={0} | all-to-all | bytes 65536 | tf_op jit(solution)/shard_map/all_to_all | solution.py:384
  16.0 5.1 %shard_map.78 = f32[32,128]{1,0:T(8,128)S(1)} custom-call(f32[64,128]{1,0:T(8,128)S(1)} %bitcast.13), custom_call_target="tpu_custom_call" | custom-call | tf_op jit(solution)/shard_map/pallas_call | solution.py:248
  21.0 8.8 %all_to_all.11 = f32[32,1,128]{2,1,0:T(1,128)S(1)} all-to-all(f32[32,1,128]{2,1,0:T(1,128)S(1)} %bitcast.15), channel_id=1, replica_groups=mesh['row'=4,'col'=8] {'row','col'}, dimensions={0} | all-to-all | bytes 32768 | tf_op jit(solution)/shard_map/all_to_all | solution.py:386
  29.8 0.7 %shard_map.79 = (f32[3,32,32]{2,1,0:T(8,128)}, f32[32,32]{1,0:T(8,128)}) custom-call(f32[32,128]{1,0:T(8,128)S(1)} %bitcast.16), custom_call_target="tpu_custom_call" | custom-call | tf_op jit(solution)/shard_map/pallas_call | solution.py:285

commit v8 on v5

--- a/solution.py
+++ b/solution.py
@@ -141,10 +141,11 @@
                 else:
                     mover = {k: moved_later[k, turn] for k in names}
                 back = None
+                here = seen(turned, turn % 13)
                 for drop in drops:
                     if turn in edges and drop > half:
                         continue
-                    stayer = {k: turned[k, drop] for k in names}
+                    stayer = {k: here[k, drop] for k in names}
                     to_mover, to_stayer = pair(mover, stayer, turn, drop)
                     stay[drop] = [a + b for a, b in zip(stay[drop], to_stayer)]
                     if turn in edges and drop in (0, half):

time: 30.7 us -> 30.9 us (level)
  no operation moved by 1% of the time
where the time goes in v8:
time: 30.9 us; the launch traced here: 30.7 us
  blocking collectives  23.1 us (75%)
  Pallas kernels  6.93 us (22%)
  between operations  0.64 us (2%)
    all_to_all x1, blocking collectives, on_device(): lax.all_to_all(packed.reshape(replicas, 2, LANES), both, split_axis=0, co...  14.3 us
    all_to_all x1, blocking collectives, on_device(): lax.all_to_all(result.reshape(replicas, 1, LANES), both, split_axis=0, co...  8.81 us
    pallas_call x1, Pallas kernels, whole_conformation(): pl.pallas_call(conformation_kernel, out_shape=jax.ShapeDtypeStruct((recv....  5.18 us
    pallas_call x1, Pallas kernels, pack(): pl.pallas_call(pack_kernel, out_shape=pltpu.VMEM((replicas * 2, LANES), j...  1.02 us
    pallas_call x1, Pallas kernels, unpack(): pl.pallas_call(unpack_kernel, out_shape=[jax.ShapeDtypeStruct(*forces), j...  0.73 us

profile of v8, /device:TPU:0, one launch (start us, length us, event | category | flops | bytes accessed | tf_op | source)
XLA Modules:
  0.0 30.7 jit_solution(12980030985549005772)
XLA Ops:
  0.6 1.0 %shard_map.77 = f32[64,128]{1,0:T(8,128)S(1)} custom-call(f32[3,32,32]{2,1,0:T(8,128)} %bitcast.17, f32[1,32]{1,0:T(1,128)} %bitcast.19, s32[1,32]{1,0:T(1,128)} %bitcast.20, s32[2,128]{1,0:T(2,128)} %bitcast.18, f32[1,32]{1,0:T(1,128)} %bitcast.21, f32[1,32]{1,0:T(1,128)} %bitcast.22), custom_call_target="tpu_custom_call" | custom-call | tf_op jit(solution)/shard_map/pallas_call | solution.py:70
  1.7 14.3 %all_to_all.10 = f32[32,2,128]{2,1,0:T(2,128)S(1)} all-to-all(f32[32,2,128]{2,1,0:T(2,128)S(1)} %bitcast.14), channel_id=1, replica_groups=mesh['row'=4,'col'=8] {'row','col'}, dimensions={0} | all-to-all | bytes 65536 | tf_op jit(solution)/shard_map/all_to_all | solution.py:392
  15.9 5.2 %shard_map.78 = f32[32,128]{1,0:T(8,128)S(1)} custom-call(f32[64,128]{1,0:T(8,128)S(1)} %bitcast.13), custom_call_target="tpu_custom_call" | custom-call | tf_op jit(solution)/shard_map/pallas_call | solution.py:255
  21.1 8.8 %all_to_all.11 = f32[32,1,128]{2,1,0:T(1,128)S(1)} all-to-all(f32[32,1,128]{2,1,0:T(1,128)S(1)} %bitcast.15), channel_id=1, replica_groups=mesh['row'=4,'col'=8] {'row','col'}, dimensions={0} | all-to-all | bytes 32768 | tf_op jit(solution)/shard_map/all_to_all | solution.py:394
  29.9 0.7 %shard_map.79 = (f32[3,32,32]{2,1,0:T(8,128)}, f32[32,32]{1,0:T(8,128)}) custom-call(f32[32,128]{1,0:T(8,128)S(1)} %bitcast.16), custom_call_target="tpu_custom_call" | custom-call | tf_op jit(solution)/shard_map/pallas_call | solution.py:293
